TPU v7x, 512 devices: a whole 4x8x8 slice. The times are simulated.
512 devices in a mesh: dp: 16 (over y_lo, z), seq: 32 (over y_hi, x, core).
Axes of the slice: x: 4, y: 8 (y_hi: 4, y_lo: 2; y = y_hi * 2 + y_lo), z: 8, core: 2. Of those that a mesh axis runs over, the one named last changes fastest.
Arguments:
- queries: bfloat16 [16, 4096, 512], P('dp', 'seq'), may hold values from -6 to 6
- keys: bfloat16 [16, 4096, 512], P('dp', 'seq'), may hold values from -6 to 6
- values: bfloat16 [16, 4096, 512], P('dp', 'seq'), may hold values from -6 to 6
- gates: bfloat16 [16, 4096, 512], P('dp', 'seq'), may hold values from -6 to 6
- out_proj: bfloat16 [512, 1024], replicated, may hold values from -0.25 to 0.25
- out_grad: bfloat16 [16, 4096, 1024], P('dp', 'seq'), may hold values from -6 to 6
- lengths: int32 [16, 4], P('dp'), may hold values from 1 to 2048, 4096 in all within a row
- rel_bias: float32 [4, 16], replicated, may hold values from -2 to 2
Outputs:
- projected: bfloat16 [16, 4096, 1024], P('dp', 'seq')
- query_grad: bfloat16 [16, 4096, 512], P('dp', 'seq')
- key_grad: bfloat16 [16, 4096, 512], P('dp', 'seq')
- value_grad: bfloat16 [16, 4096, 512], P('dp', 'seq')
- bias_grad: float32 [4, 16], replicated
Inputs may be any that keep to these rules, and one draw needn't show every extreme that they name: In every data row the 4 lengths sum to 4096 and the longest is exactly half of 4096.
All inputs are finite; a program needn't handle non-finite values.
Results may differ from a plain program's by a relative error of at most 0.0059.
Values may be sent and summed in bfloat16 or wider, within the bound.
A program may use at most 64 MiB of HBM per device.

v0:
```python
import math

import jax
import jax.numpy as jnp
from jax import lax
from jax.sharding import PartitionSpec as P

epsilon = 1e-05


def positions_and_segments(lengths_row, first_row, row_total):
    ends = jnp.cumsum(lengths_row)
    where_at = first_row + jnp.arange(row_total, dtype=jnp.int32)
    segment = jnp.sum((where_at[:, None] >= ends[None, :]).astype(jnp.int32), axis=1)
    return (where_at, segment)


def segment_bounds(lengths_row, segment_id):
    ends = jnp.cumsum(lengths_row)
    starts = ends - lengths_row
    picked = jnp.arange(lengths_row.shape[0], dtype=jnp.int32) == segment_id
    return (jnp.sum(jnp.where(picked, starts, 0)), jnp.sum(jnp.where(picked, ends, 0)))


def pair_scores(query_block, query_pos, query_seg, key_block, key_pos, key_seg, rel_bias):
    head_width = query_block.shape[2]
    products = jnp.einsum(
        "qhd,khd->hqk", query_block, key_block, preferred_element_type=jnp.float32
    )
    distance = query_pos[:, None] - key_pos[None, :]
    bucket = jnp.zeros(distance.shape, jnp.int32)
    for octave in range(15):
        bucket = bucket + (distance >= 2**octave).astype(jnp.int32)
    one_hot = (bucket[:, :, None] == jnp.arange(rel_bias.shape[1], dtype=jnp.int32)).astype(
        jnp.float32
    )
    shifted = jnp.einsum("hb,qkb->hqk", rel_bias, one_hot, precision=lax.Precision.HIGHEST)
    scores = products * head_width ** (-0.5) + shifted
    allowed = ((query_seg[:, None] == key_seg[None, :]) & (distance >= 0))[None]
    return (scores, allowed, one_hot)


def over_blocks(step_fn, live_fn, running, arrays, first_row):
    row_total = arrays[0].shape[0]
    block_rows = math.gcd(row_total, 512)
    block_count = row_total // block_rows
    stacked = tuple(
        (member.reshape((block_count, block_rows) + member.shape[1:]) for member in arrays)
    )

    def advance(partial_sum, element):
        block_index, pieces = element
        block_first = first_row + block_index * block_rows
        updated = lax.cond(
            live_fn(block_first, block_rows),
            lambda state: step_fn(state, pieces, block_first),
            lambda state: state,
            partial_sum,
        )
        return (updated, None)

    result, unused = lax.scan(advance, running, (jnp.arange(block_count, dtype=jnp.int32), stacked))
    return result


def shards(queries, keys, values, gates, out_proj, out_grad, lengths, rel_bias):
    heads = rel_bias.shape[0]
    tok_rows = queries.shape[1]
    feature_width = queries.shape[2]
    head_width = feature_width // heads
    own_queries = queries[0].reshape(tok_rows, heads, head_width)
    own_keys = keys[0].reshape(tok_rows, heads, head_width)
    own_values = values[0].reshape(tok_rows, heads, head_width)
    own_gates = gates[0].reshape(tok_rows, heads, head_width)
    lengths_row = lengths[0]
    own_first = lax.axis_index("seq") * tok_rows
    own_last = own_first + tok_rows - 1
    own_pos, own_seg = positions_and_segments(lengths_row, own_first, tok_rows)
    earliest_start, unused_end = segment_bounds(lengths_row, own_seg[0])
    unused_start, latest_end = segment_bounds(lengths_row, own_seg[tok_rows - 1])
    zero_heads = jnp.zeros((tok_rows, heads, head_width), jnp.float32)

    def keys_live(block_first, count):
        return (block_first <= own_last) & (block_first + count > earliest_start)

    def queries_live(block_first, count):
        return (block_first + count > own_first) & (block_first < latest_end)

    def forward_step(running, pieces, first_row):
        key_block, value_block = pieces
        key_pos, key_seg = positions_and_segments(lengths_row, first_row, key_block.shape[0])
        scores, allowed, one_hot = pair_scores(
            own_queries, own_pos, own_seg, key_block, key_pos, key_seg, rel_bias
        )
        weights = jnp.where(allowed, jax.nn.silu(scores), 0.0).astype(jnp.bfloat16)
        return running + jnp.einsum(
            "hqk,khd->qhd", weights, value_block, preferred_element_type=jnp.float32
        )

    all_keys, all_values = (
        lax.all_gather(own_keys, "seq", axis=0, tiled=True),
        lax.all_gather(own_values, "seq", axis=0, tiled=True),
    )
    mixed = over_blocks(forward_step, keys_live, zero_heads, (all_keys, all_values), 0)
    average = jnp.mean(mixed, axis=2, keepdims=True)
    centred = mixed - average
    variance = jnp.mean(centred * centred, axis=2, keepdims=True)
    inverse = lax.rsqrt(variance + epsilon)
    normed = centred * inverse
    gated = (
        (normed * own_gates.astype(jnp.float32))
        .astype(jnp.bfloat16)
        .reshape(tok_rows, feature_width)
    )
    projected = jnp.dot(gated, out_proj, preferred_element_type=jnp.float32).astype(jnp.bfloat16)
    gated_grad = jnp.einsum("te,ce->tc", out_grad[0], out_proj, preferred_element_type=jnp.float32)
    normed_grad = gated_grad.reshape(tok_rows, heads, head_width) * own_gates.astype(jnp.float32)
    mixed_grad = (
        normed_grad
        - jnp.mean(normed_grad, axis=2, keepdims=True)
        - normed * jnp.mean(normed_grad * normed, axis=2, keepdims=True)
    ) * inverse
    mixed_grad = mixed_grad.astype(jnp.bfloat16)

    def query_step(running, pieces, first_row):
        key_block, value_block = pieces
        key_pos, key_seg = positions_and_segments(lengths_row, first_row, key_block.shape[0])
        scores, allowed, one_hot = pair_scores(
            own_queries, own_pos, own_seg, key_block, key_pos, key_seg, rel_bias
        )
        sigmoid_s = jax.nn.sigmoid(scores)
        attn_grad = jnp.einsum(
            "qhd,khd->hqk", mixed_grad, value_block, preferred_element_type=jnp.float32
        )
        score_grad = jnp.where(
            allowed, attn_grad * sigmoid_s * (1.0 + scores * (1.0 - sigmoid_s)), 0.0
        )
        score_low = score_grad.astype(jnp.bfloat16)
        return running + jnp.einsum(
            "hqk,khd->qhd", score_low, key_block, preferred_element_type=jnp.float32
        )

    def key_step(running, pieces, first_row):
        key_total, value_total, bias_part = running
        query_block, grad_block = pieces
        query_pos, query_seg = positions_and_segments(lengths_row, first_row, query_block.shape[0])
        scores, allowed, one_hot = pair_scores(
            query_block, query_pos, query_seg, own_keys, own_pos, own_seg, rel_bias
        )
        sigmoid_s = jax.nn.sigmoid(scores)
        weights = jnp.where(allowed, scores * sigmoid_s, 0.0).astype(jnp.bfloat16)
        attn_grad = jnp.einsum(
            "qhd,khd->hqk", grad_block, own_values, preferred_element_type=jnp.float32
        )
        score_grad = jnp.where(
            allowed, attn_grad * sigmoid_s * (1.0 + scores * (1.0 - sigmoid_s)), 0.0
        )
        score_low = score_grad.astype(jnp.bfloat16)
        key_total = key_total + jnp.einsum(
            "hqk,qhd->khd", score_low, query_block, preferred_element_type=jnp.float32
        )
        value_total = value_total + jnp.einsum(
            "hqk,qhd->khd", weights, grad_block, preferred_element_type=jnp.float32
        )
        bias_terms = jnp.einsum("hqk,qkb->hb", score_grad, one_hot, precision=lax.Precision.HIGHEST)
        return (key_total, value_total, bias_part + bias_terms)

    first_row = jnp.int32(0)
    query_total = zero_heads
    key_total = zero_heads
    value_total = zero_heads
    bias_part = jnp.zeros(rel_bias.shape, jnp.float32)
    query_piece = lax.all_gather(own_queries, "seq", axis=0, tiled=True)
    grad_piece = lax.all_gather(mixed_grad, "seq", axis=0, tiled=True)
    key_piece = lax.all_gather(own_keys, "seq", axis=0, tiled=True)
    value_piece = lax.all_gather(own_values, "seq", axis=0, tiled=True)
    query_total = over_blocks(
        query_step, keys_live, query_total, (key_piece, value_piece), first_row
    )
    key_total, value_total, bias_part = over_blocks(
        key_step,
        queries_live,
        (key_total, value_total, bias_part),
        (query_piece, grad_piece),
        first_row,
    )
    query_total, key_total, value_total, bias_part = (
        query_total,
        key_total,
        value_total,
        bias_part,
    )
    bias_grad = lax.psum(bias_part, ("dp", "seq"))
    query_grad = query_total.reshape(1, tok_rows, feature_width).astype(jnp.bfloat16)
    key_grad = key_total.reshape(1, tok_rows, feature_width).astype(jnp.bfloat16)
    value_grad = value_total.reshape(1, tok_rows, feature_width).astype(jnp.bfloat16)
    return (projected[None], query_grad, key_grad, value_grad, bias_grad)


def solution(mesh):
    in_specs = (
        P("dp", "seq", None),
        P("dp", "seq", None),
        P("dp", "seq", None),
        P("dp", "seq", None),
        P(),
        P("dp", "seq", None),
        P("dp", None),
        P(),
    )
    out_specs = (
        P("dp", "seq", None),
        P("dp", "seq", None),
        P("dp", "seq", None),
        P("dp", "seq", None),
        P(),
    )
    return jax.shard_map(shards, mesh=mesh, in_specs=in_specs, out_specs=out_specs, check_vma=False)
```

profile of v0, /device:TPU:1, one launch (start us, length us, event | category | flops | bytes accessed | tf_op | source)
XLA Modules:
  0.0 500.7 jit_solution(6191673273034674706)
XLA Ops:
  7.2 1.7 copy.79
  9.0 1.7 copy.81
  10.8 1.7 copy.80
  14.4 1.7 copy.86
  16.8 2.7 fusion.98
  19.5 68.8 %all-gather.5.cloned.1.call-done = bf16[4096,4,128]{0,2,1:T(8,128)(2,1)} async-done(((bf16[128,4,128]{0,2,1:T(8,128)(2,1)}), bf16[4096,4,128]{0,2,1:T(8,128)(2,1)}) %all-gather.5.cloned.1.call-update) | async-done | bytes 4194320 | tf_op jit(solution)/shard_map/all_gather | solution.py:101
  88.3 6.4 %copy.103 = bf16[64,8,8,512]{3,2,1,0:T(8,128)(2,1)} copy(bf16[64,8,8,512]{3,1,2,0:T(8,128)(2,1)} %bitcast.164) | data formatting | bytes 8388608
  94.6 7.9 %copy.82 = bf16[8,512,4,128]{3,1,2,0:T(8,128)(2,1)} copy(bf16[8,512,4,128]{1,0,3,2:T(8,128)(2,1)} %bitcast.159) | data formatting | bytes 8388608
  102.6 58.8 %all-gather.7.cloned.1.call-done = bf16[4096,4,128]{0,2,1:T(8,128)(2,1)} async-done(((bf16[128,4,128]{0,2,1:T(8,128)(2,1)}), bf16[4096,4,128]{0,2,1:T(8,128)(2,1)}) %all-gather.7.cloned.1.call-update) | async-done | bytes 4194320 | tf_op jit(solution)/shard_map/all_gather | solution.py:102
  161.3 6.4 %copy.104 = bf16[64,8,8,512]{3,2,1,0:T(8,128)(2,1)} copy(bf16[64,8,8,512]{3,1,2,0:T(8,128)(2,1)} %bitcast.165) | data formatting | bytes 8388608
  167.7 7.9 %copy.84 = bf16[8,512,4,128]{3,1,2,0:T(8,128)(2,1)} copy(bf16[8,512,4,128]{1,0,3,2:T(8,128)(2,1)} %bitcast.160) | data formatting | bytes 8388608
  176.2 25.5 %while.44 = (s32[]{:T(128)}, f32[128,4,128]{2,0,1:T(8,128)S(1)}, s32[8]{0:T(128)}, s32[]{:T(128)}, s32[]{:T(128)}, /*index=5*/s32[128]{0:T(128)S(1)}, s32[4]{0:T...) while((s32[]{:T(128)}, f32[128,4,128]{2,0,1:T(8,128)S(1)}, ...), condition=%wide.region_8.9_spmd.clone, body=%wide.region_3.8_spmd.clone.sunk | while | flops 190978192 | bytes 7094895 | solution.py:62
  178.7 5.4 %conditional.10 = (f32[128,4,128]{2,0,1:T(8,128)S(1)}) conditional(s32[]{:T(128)} %convert_element_type.601, f32[128,4,128]{2,0,1:T(8,128)S(1)} %get-tuple-element.1113, (s32[128]{0:T(128)S(1)}, s32[]{:T(128)}, s32[4]{0:T(128)}, s32[]{:T(128)}, bf16[8,512,4,128]{3,1,2,0:T(8,128)(2,1)}, /*index=5*/s32[]{:T(128)}, bf16[128,4,128]{2,0,1:T(8,128)(2,1)S(1)}, ...), branch_computations={%region_4.4_spmd, %region_5.7_spmd} | conditional | flops 190978192 | bytes 7094084 | solution.py:54
  179.3 1.3 fusion.6
  182.2 2.0 fusion.10
  202.1 1.5 fusion.99
  203.6 1.7 multiply_convert_fusion
  206.2 1.7 copy.88
  209.1 27.4 %while.45 = (s32[]{:T(128)}, f32[128,4,128]{2,0,1:T(8,128)}, s32[8]{0:T(128)}, s32[]{:T(128)}, s32[]{:T(128)}, /*index=5*/s32[128]{0:T(128)S(1)}, s32[4]{0:T(128...) while((s32[]{:T(128)}, f32[128,4,128]{2,0,1:T(8,128)}, ...), condition=%wide.region_18.19_spmd.clone, body=%wide.region_13.18_spmd.clone.sunk | while | flops 259135632 | bytes 9847935 | solution.py:62
  211.6 7.6 %conditional.11 = (f32[128,4,128]{2,0,1:T(8,128)}) conditional(s32[]{:T(128)} %convert_element_type.602, f32[128,4,128]{2,0,1:T(8,128)} %get-tuple-element.1159, (s32[128]{0:T(128)S(1)}, s32[]{:T(128)}, s32[4]{0:T(128)}, s32[]{:T(128)}, bf16[8,512,4,128]{3,1,2,0:T(8,128)(2,1)}, /*index=5*/s32[]{:T(128)}, bf16[128,4,128]{2,0,1:T(8,128)(2,1)}, ...), branch_computations={%region_14.14_spmd, %region_15.17_spmd} | conditional | flops 259135632 | bytes 9847108 | solution.py:54
  213.9 1.3 fusion.31
  216.4 2.8 fusion.38
  238.4 6.3 %copy.92 = bf16[4096,4,128]{2,0,1:T(8,128)(2,1)} copy(bf16[4096,4,128]{0,2,1:T(8,128)(2,1)} %all-gather.11.cloned.1.call-done) | data formatting | bytes 8388608 | tf_op jit(solution)/shard_map/all_gather | solution.py:173
  244.7 4.6 copy.95
  250.3 56.3 %all-gather.9.cloned.1.call-done = bf16[4096,4,128]{0,2,1:T(8,128)(2,1)} async-done(((bf16[128,4,128]{0,2,1:T(8,128)(2,1)}), bf16[4096,4,128]{0,2,1:T(8,128)(2,1)}) %all-gather.9.cloned.1.call-update) | async-done | bytes 4194320 | tf_op jit(solution)/shard_map/all_gather | solution.py:174
  306.6 6.4 %copy.105 = bf16[64,8,8,512]{3,2,1,0:T(8,128)(2,1)} copy(bf16[64,8,8,512]{3,1,2,0:T(8,128)(2,1)} %bitcast.163) | data formatting | bytes 8388608
  313.0 8.0 %copy.93 = bf16[8,512,4,128]{3,1,2,0:T(8,128)(2,1)} copy(bf16[8,512,4,128]{1,0,3,2:T(8,128)(2,1)} %bitcast.162) | data formatting | bytes 8388608
  321.1 51.8 %while.46 = (s32[]{:T(128)}, f32[128,4,128]{2,0,1:T(8,128)S(1)}, f32[128,4,128]{2,0,1:T(8,128)S(1)}, f32[4,16]{1,0:T(4,128)S(1)}, s32[8]{0:T(128)S(1)}, /*index=...) while((s32[]{:T(128)}, f32[128,4,128]{2,0,1:T(8,128)S(1)}, ...), condition=%wide.region_25.26_spmd.clone.clone, body=%wide.region_20.25_spmd.clone.clone.sunk | while | flops 379263168 | bytes 17516744 | solution.py:62
  323.0 12.2 %conditional.12 = ((f32[128,4,128]{2,0,1:T(8,128)S(1)}, f32[128,4,128]{2,0,1:T(8,128)S(1)}, f32[4,16]{1,0:T(4,128)S(1)})) conditional(s32[]{:T(128)} %convert_element_type.603, (f32[128,4,128]{2,0,1:T(8,128)S(1)}, f32[128,4,128]{2,0,1:T(8,128)S(1)}, f32[4,16]{1,0:T(4,128)S(1)}) %tuple.118, (s32[]{:T(128)}, s32[4]{0:T(128)S(1)}, s32[128]{0:T(128)S(1)}, ...), branch_computations={%region_21.21_spmd, %region_22.24_spmd} | conditional | flops 379263168 | bytes 17515868 | solution.py:54
  325.3 1.3 fusion.68
  327.1 1.6 fusion.70
  328.7 1.4 fusion.71
  330.2 1.6 fusion.72
  332.3 2.9 fusion.74
  337.0 12.2 %conditional.12 = ((f32[128,4,128]{2,0,1:T(8,128)S(1)}, f32[128,4,128]{2,0,1:T(8,128)S(1)}, f32[4,16]{1,0:T(4,128)S(1)})) conditional(s32[]{:T(128)} %convert_element_type.603, (f32[128,4,128]{2,0,1:T(8,128)S(1)}, f32[128,4,128]{2,0,1:T(8,128)S(1)}, f32[4,16]{1,0:T(4,128)S(1)}) %tuple.118, (s32[]{:T(128)}, s32[4]{0:T(128)S(1)}, s32[128]{0:T(128)S(1)}, ...), branch_computations={%region_21.21_spmd, %region_22.24_spmd} | conditional | flops 379263168 | bytes 17515868 | solution.py:54
  339.4 1.3 fusion.68
  341.2 1.6 fusion.70
  342.8 1.4 fusion.71
  344.2 1.6 fusion.72
  346.3 2.9 fusion.74
  351.1 12.2 %conditional.12 = ((f32[128,4,128]{2,0,1:T(8,128)S(1)}, f32[128,4,128]{2,0,1:T(8,128)S(1)}, f32[4,16]{1,0:T(4,128)S(1)})) conditional(s32[]{:T(128)} %convert_element_type.603, (f32[128,4,128]{2,0,1:T(8,128)S(1)}, f32[128,4,128]{2,0,1:T(8,128)S(1)}, f32[4,16]{1,0:T(4,128)S(1)}) %tuple.118, (s32[]{:T(128)}, s32[4]{0:T(128)S(1)}, s32[128]{0:T(128)S(1)}, ...), branch_computations={%region_21.21_spmd, %region_22.24_spmd} | conditional | flops 379263168 | bytes 17515868 | solution.py:54
  351.8 1.3 fusion.65
  353.5 1.3 fusion.68
  355.3 1.6 fusion.70
  356.9 1.4 fusion.71
  358.3 1.6 fusion.72
  360.4 2.9 fusion.74
  374.6 119.5 %psum.7 = f32[4,16]{1,0:T(4,128)} all-reduce(f32[4,16]{1,0:T(4,128)S(1)} %get-tuple-element.505), channel_id=1, replica_groups=mesh['dp'=16,'seq'=32] {'dp','seq'}, use_global_device_ids=true, to_apply=%region_26.27 | all-reduce | flops 64 | bytes 512 | tf_op jit(solution)/shard_map/psum | solution.py:193
  (167 shorter events, 49.7 us)
Async XLA Ops:
  7.2 194.9 %copy-start = (bf16[512,1024]{1,0:T(8,128)(2,1)S(1)}, bf16[512,1024]{1,0:T(8,128)(2,1)}, u32[]{:S(2)}) copy-start(bf16[512,1024]{1,0:T(8,128)(2,1)} %param.24) | copy-start | bytes 3145732
  7.2 81.1 %all-gather.5.cloned.1.call-start = ((), (), s32[]{:S(2)}) async-start(), calls=%async_computation | async-start | bytes 4325376 | tf_op jit(solution)/shard_map/all_gather | solution.py:101
  9.0 152.3 %all-gather.7.cloned.1.call-start = ((), (), s32[]{:S(2)}) async-start(), calls=%async_computation.1 | async-start | bytes 4325376 | tf_op jit(solution)/shard_map/all_gather | solution.py:102
  10.7 227.6 %all-gather.11.cloned.1.call-start = ((), (), s32[]{:S(2)}) async-start(), calls=%async_computation.3 | async-start | bytes 4325376 | tf_op jit(solution)/shard_map/all_gather | solution.py:173
  12.5 294.2 %all-gather.9.cloned.1.call-start = ((), (), s32[]{:S(2)}) async-start(), calls=%async_computation.2 | async-start | bytes 4325376 | tf_op jit(solution)/shard_map/all_gather | solution.py:174
  167.7 8.5 %copy-start.4 = (f32[4,16]{1,0:T(4,128)S(1)}, f32[4,16]{1,0:T(4,128)}, u32[]{:S(2)}) copy-start(f32[4,16]{1,0:T(4,128)} %param.27) | copy-start | bytes 772
  201.7 3.6 copy-start.3
  201.7 4.4 copy-start.2
  313.0 8.0 %copy-start.5 = (bf16[128,4,128]{2,0,1:T(8,128)(2,1)S(1)}, bf16[128,4,128]{2,0,1:T(8,128)(2,1)}, u32[]{:S(2)}) copy-start(bf16[128,4,128]{2,0,1:T(8,128)(2,1)} %copy.94) | copy-start | bytes 393220
  313.0 8.0 %copy-start.6 = (s32[4]{0:T(128)S(1)}, s32[4]{0:T(128)}, u32[]{:S(2)}) copy-start(s32[4]{0:T(128)} %get-tuple-element.1271) | copy-start | bytes 52
  372.9 121.2 %copy-start.1 = (bf16[512,1024]{1,0:T(8,128)(2,1)S(1)}, bf16[512,1024]{1,0:T(8,128)(2,1)}, u32[]{:S(2)}) copy-start(bf16[512,1024]{1,0:T(8,128)(2,1)} %param.24) | copy-start | bytes 3145732
Sparse Core Ops, SparseCore 0:
  11.6 76.5 all-gather.4
  91.9 69.3 all-gather.6
  165.0 69.4 all-gather.10
  237.3 69.2 all-gather.8
where the time goes:
time: 504 us; the launch traced here: 501 us
  waiting for transfers between devices  184 us (37%)
  blocking collectives  119 us (24%)
  local copies, waits for them, and re-layouts  98.5 us (20%)
  matrix products  41.5 us (8%)
  loops' own time  30.6 us (6%)
  between operations  14 us (3%)
  other arithmetic  12.4 us (2%)
    psum x1, blocking collectives, shards(): bias_grad = lax.psum(bias_part, ('dp', 'seq'))  119 us
    all_gather x1, waiting for transfers between devices, shards(): lax.all_gather(own_keys, 'seq', axis=0, tiled=True)  68.8 us
    all_gather x1, waiting for transfers between devices, shards(): lax.all_gather(own_values, 'seq', axis=0, tiled=True)  58.8 us
    all_gather x1, waiting for transfers between devices, shards(): grad_piece = lax.all_gather(mixed_grad, 'seq', axis=0, tiled=True)  56.3 us
    unnamed x28, local copies, waits for them, and re-layouts  56.2 us
    another operation x3, loops' own time, over_blocks(): lax.scan(advance, running, (jnp.arange(block_count, dtype=jnp.int32), sta...  29.9 us
    dynamic_slice x24, local copies, waits for them, and re-layouts, over_blocks(): lax.scan(advance, running, (jnp.arange(block_count, dtype=jnp.int32), sta...  24.9 us
  transfers between devices with their start and end apart: 4, of which 3 were waited for; matrix products, arithmetic and copies ran while one was open for 19% of the time, Pallas kernels for 0%

commit v1 on v0

v1 whole, which is shorter than its diff:
```python
import jax
import jax.numpy as jnp
from jax import lax
from jax.experimental import pallas as pl
from jax.experimental.pallas import tpu as pltpu
from jax.sharding import PartitionSpec as P

F32 = jnp.float32
BF16 = jnp.bfloat16
EPS = 1e-05
NEG = -1e5
HALF_SCALE = 0.5 * 128 ** (-0.5)
FAR = 1 << 20
TABLED = (0, 1, 2, 4)
LEFT, DIAG, RIGHT = 1, 2, 3


def dot_nt(a, b):
    return lax.dot_general(a, b, (((1,), (1,)), ((), ())), preferred_element_type=F32)


def dot_nn(a, b):
    return jnp.dot(a, b, preferred_element_type=F32)


def kernel(
    q_in, k_in, v_in, gates_in, proj_in, og_in, len_ref, rb_ref,
    projected_ref, dq_ref, dk_ref, dv_ref, bias_ref,
    kbuf, vbuf, qbuf, gbuf, ngbuf, ngsrc, nrmsrc, nrmbuf, lensrc, lenbuf,
    og_vm, gates_vm, proj_vm, gated_vm, outproj_vm,
    tab_q, tab_k, st_t, en_t, acc_m, acc_q, acc_k, acc_v,
    out_q, out_k, out_v, acc_bias, acc_far, red,
    send_sems, y_sems, x_sems, ret_sems, red_sems, len_sem, local_sems,
):
    dp = lax.axis_index("dp")
    seq = lax.axis_index("seq")
    ylo, z = lax.div(dp, 8), lax.rem(dp, 8)
    yh, xc = lax.div(seq, 8), lax.rem(seq, 8)
    x, c = lax.div(xc, 2), lax.rem(xc, 2)
    odp = lax.rem(dp + 8, 16)
    yi = ylo * 4 + yh

    def place(rel):
        return lax.rem(x + rel, 4)

    left, right, diag = place(3), place(1), place(2)
    dev_left = (dp, yh * 8 + left * 2 + c)
    dev_right = (dp, yh * 8 + right * 2 + c)
    dev_sib = (dp, yh * 8 + x * 2 + 1 - c)

    def z_partner(k):
        other = lax.rem(z + k, 8)
        return (ylo * 8 + other, seq), other

    def xc_partner(k):
        other = lax.rem(xc + k, 8)
        return (dp, yh * 8 + other), other

    def y_partner(k):
        other = lax.rem(yi + k, 8)
        return (lax.div(other, 4) * 8 + z, lax.rem(other, 4) * 8 + xc), other

    partners = (z_partner, xc_partner, y_partner)

    barrier = pltpu.get_barrier_semaphore()
    for partner in (y_partner, xc_partner, z_partner):
        for k in range(1, 8):
            pl.semaphore_signal(
                barrier, inc=1, device_id=partner(k)[0], device_id_type=pl.DeviceIdType.MESH
            )

    local = [
        pltpu.make_async_copy(og_in.at[0], og_vm, local_sems.at[0]),
        pltpu.make_async_copy(proj_in, proj_vm, local_sems.at[1]),
        pltpu.make_async_copy(gates_in.at[0], gates_vm, local_sems.at[2]),
    ]
    ends = []
    total = len_ref[0, 0]
    ends.append(total)
    for u in range(1, 4):
        total = total + len_ref[0, u]
        ends.append(total)
    row_at = lax.broadcasted_iota(jnp.int32, (8, 128), 0)
    end_rows = jnp.zeros((8, 128), F32)
    for u in range(4):
        end_rows = jnp.where(row_at == u, ends[u].astype(F32), end_rows)
    lensrc[...] = end_rows

    pending = []

    def send(src, dst, recv_sem, dev):
        copy = pltpu.make_async_remote_copy(
            src_ref=src, dst_ref=dst, send_sem=send_sems.at[len(pending)], recv_sem=recv_sem,
            device_id=dev, device_id_type=pl.DeviceIdType.MESH,
        )
        copy.start()
        pending.append(copy)

    def arrived(dst, sem):
        pltpu.make_async_copy(dst, dst, sem).wait()

    pl.semaphore_wait(barrier, 21)

    def y_send(a, src_of, dst):
        for h in range(4):
            send(src_of(h), dst, y_sems.at[a, yh], (odp, h * 8 + xc))

    def y_wait(a, dst_of):
        for s in range(4):
            arrived(dst_of(s), y_sems.at[a, s])

    for a, (src, buf) in enumerate(((k_in, kbuf), (v_in, vbuf), (q_in, qbuf))):
        y_send(a, lambda h, src=src: src.at[0, :, h * 128 : (h + 1) * 128], buf.at[yh, xc])
        if a == 0:
            send(lensrc, lenbuf, len_sem.at[0], (odp, seq))
    for copy in local:
        copy.start()

    def piece(buf, half, at):
        return buf.at[pl.ds(2 * half, 2), at]

    def own_of(at):
        return at * 2 + c

    def x_start(a, buf):
        mine = own_of(x)
        send(piece(buf, 0, mine), piece(buf, 0, mine), x_sems.at[a, 0], dev_right)
        send(piece(buf, 1, mine), piece(buf, 1, mine), x_sems.at[a, 3], dev_left)
        send(piece(buf, 1, mine), piece(buf, 1, mine), x_sems.at[a, 1], dev_right)
        send(piece(buf, 0, mine), piece(buf, 0, mine), x_sems.at[a, 4], dev_left)
        send(buf.at[:, mine], buf.at[:, mine], x_sems.at[a, 6], dev_sib)

    def x_pass(a, buf, steps):
        for half, whose, slot, to in steps:
            part = piece(buf, half, own_of(whose))
            arrived(part, x_sems.at[a, slot])
            if to is not None:
                device, next_slot = to
                send(part, part, x_sems.at[a, next_slot], device)
            send(part, part, x_sems.at[a, slot + 7], dev_sib)

    def x_near(a, buf):
        x_pass(a, buf, ((0, left, 0, (dev_right, 2)), (1, right, 3, (dev_left, 5))))

    def x_rest(a, buf):
        x_pass(a, buf, ((1, left, 1, None), (0, right, 4, None)))

    def x_far(a, buf):
        x_pass(a, buf, ((0, diag, 2, None), (1, diag, 5, None)))

    def sib_of(at):
        return at * 2 + 1 - c

    def sib_own(a, buf):
        arrived(buf.at[:, sib_of(x)], x_sems.at[a, 6])

    def sib_near(a, buf):
        arrived(piece(buf, 0, sib_of(left)), x_sems.at[a, 7])
        arrived(piece(buf, 1, sib_of(right)), x_sems.at[a, 10])
        arrived(piece(buf, 1, sib_of(left)), x_sems.at[a, 8])
        arrived(piece(buf, 0, sib_of(right)), x_sems.at[a, 11])

    def sib_far(a, buf):
        arrived(piece(buf, 0, sib_of(diag)), x_sems.at[a, 9])
        arrived(piece(buf, 1, sib_of(diag)), x_sems.at[a, 12])

    wide = (128, 256)
    sub = lax.broadcasted_iota(jnp.int32, wide, 0)
    lane = lax.broadcasted_iota(jnp.int32, wide, 1)
    dist_q = 128 * c + sub - lane
    dist_k = lane - sub - 128 * c
    half_bias = [0.5 * rb_ref[yh, b] for b in range(12)]

    def biases(dist, low, high):
        filled = jnp.full(wide, half_bias[low], F32)
        for b in range(low + 1, high + 1):
            filled = jnp.where(dist >= 2 ** (b - 1), half_bias[b], filled)
        return filled

    spans = {0: (0, 9), 1: (1, 9), 2: (9, 10), 4: (10, 11)}

    def build_tables():
        for tab, dist in ((tab_q, dist_q), (tab_k, dist_k)):
            for at, d in enumerate(TABLED):
                filled = biases(dist + 256 * d, *spans[d])
                if d == 0:
                    filled = jnp.where(dist >= 0, filled, NEG)
                tab[at] = filled

    def bias_at(tab, d):
        if d in TABLED:
            return tab[TABLED.index(d)]
        return half_bias[10 if d == 3 else 11]

    def build_bounds():
        arrived(lenbuf, len_sem.at[0])
        sub_f, lane_f = sub.astype(F32), lane.astype(F32)
        ends_at = [jnp.broadcast_to(lenbuf[u : u + 1, 0:1], wide) for u in range(4)]
        for y in range(4):
            pos = sub_f + ((8 * y + xc) * 128).astype(F32)
            start = jnp.zeros(wide, F32)
            end = ends_at[3]
            for u in (0, 1, 2):
                start = jnp.where(pos >= ends_at[u], ends_at[u], start)
            for u in (2, 1, 0):
                end = jnp.where(pos < ends_at[u], ends_at[u], end)
            st_t[y] = start - lane_f
            en_t[y] = end - lane_f

    def gate_grads():
        for copy in local:
            copy.wait()
        gg = dot_nt(og_vm[...], proj_vm[...])
        ng = gg * gates_vm[...].astype(F32)
        for h in range(4):
            ngsrc[h] = ng[:, h * 128 : (h + 1) * 128]
        y_send(3, lambda h: ngsrc.at[h], ngbuf.at[yh])

    def pair(buf, y, at):
        return buf[y, pl.ds(at * 2, 2)].reshape(256, 128)

    def query_tiles(r):
        at = lax.rem(x - r + 4, 4)
        wrap = 1 - lax.div(x - r + 4, 4)
        for y in range(4):
            tiles = []
            for j in range(3 if r == 0 else 2):
                if y < j:
                    continue
                if r == 0:
                    ky, off = y - j, 0
                else:
                    ky, off = lax.rem(y - wrap - j + 4, 4), (wrap * FAR if y == j else 0)
                first = ((4 * ky + at) * 256 - off).astype(F32)
                tiles.append((r + 4 * j, ky, first))
            yield y, at, tiles

    def key_tiles(r):
        at = lax.rem(x + r, 4)
        wrap = lax.div(x + r, 4)
        for y in range(4):
            tiles = []
            for j in range(3 if r == 0 else 2):
                if y + j > 3:
                    continue
                if r == 0:
                    qy, off = y + j, 0
                else:
                    qy, off = lax.rem(y + wrap + j, 4), (wrap * FAR if y + j == 3 else 0)
                first = ((4 * qy + at) * 256 + off).astype(F32)
                tiles.append((r + 4 * j, qy, first))
            yield y, at, tiles

    def forward(r):
        for y, at, tiles in query_tiles(r):
            part = None if r == 0 else acc_m[y]
            for d, ky, first in tiles:
                s = dot_nt(qbuf[y, xc], pair(kbuf, ky, at))
                t = s * HALF_SCALE + bias_at(tab_q, d)
                t = jnp.where(st_t[y] <= first, t, NEG)
                w = (t * jnp.tanh(t) + t).astype(BF16)
                add = dot_nn(w, pair(vbuf, ky, at))
                part = add if part is None else part + add
            acc_m[y] = part

    def fold(ds):
        return jnp.sum(ds.reshape(16, 8, 256), axis=0)

    def query_grads(r):
        sums = {}
        for y, at, tiles in query_tiles(r):
            part = None if r == 0 else acc_q[y]
            for d, ky, first in tiles:
                keys = pair(kbuf, ky, at)
                s = dot_nt(qbuf[y, xc], keys)
                t = s * HALF_SCALE + bias_at(tab_q, d)
                t = jnp.where(st_t[y] <= first, t, NEG)
                th = jnp.tanh(t)
                ds = dot_nt(gbuf[y, xc], pair(vbuf, ky, at)) * ((1.0 + th) * (1.0 + t * (1.0 - th)))
                if d in TABLED:
                    slot = acc_bias.at[TABLED.index(d)]
                    slot[...] = ds if d not in sums else slot[...] + ds
                else:
                    slot = acc_far.at[(3, 5, 6, 7, 8).index(d)]
                    slot[...] = fold(ds) if d not in sums else slot[...] + fold(ds)
                sums[d] = True
                add = dot_nn(ds.astype(BF16), keys)
                part = add if part is None else part + add
            acc_q[y] = part

    def key_grads(r):
        for y, at, tiles in key_tiles(r):
            key_part = None if r == 0 else acc_k[y]
            value_part = None if r == 0 else acc_v[y]
            for d, qy, first in tiles:
                queries, grads = pair(qbuf, qy, at), pair(gbuf, qy, at)
                s = dot_nt(kbuf[y, xc], queries)
                t = s * HALF_SCALE + bias_at(tab_k, d)
                t = jnp.where(en_t[y] > first, t, NEG)
                th = jnp.tanh(t)
                one = 1.0 + th
                w = (t * one).astype(BF16)
                ds = dot_nt(vbuf[y, xc], grads) * (one * (1.0 + t * (1.0 - th)))
                add_k = dot_nn(ds.astype(BF16), queries)
                add_v = dot_nn(w, grads)
                key_part = add_k if key_part is None else key_part + add_k
                value_part = add_v if value_part is None else value_part + add_v
            acc_k[y] = key_part
            acc_v[y] = value_part

    def own_cols(h):
        return pl.ds(pl.multiple_of(h * 128, 128), 128)

    def give_back(a, src, out_ref):
        for y in range(4):
            send(
                src.at[y], out_ref.at[0, :, own_cols(yh)], ret_sems.at[a, yh], (odp, y * 8 + xc)
            )

    y_wait(0, lambda s: kbuf.at[s, xc])
    x_start(0, kbuf)
    gate_grads()
    y_wait(1, lambda s: vbuf.at[s, xc])
    x_start(1, vbuf)
    x_near(0, kbuf)
    build_tables()
    x_rest(0, kbuf)
    y_wait(2, lambda s: qbuf.at[s, xc])
    x_start(2, qbuf)
    x_near(1, vbuf)
    x_far(0, kbuf)
    build_bounds()
    sib_own(0, kbuf)
    sib_own(1, vbuf)
    forward(0)
    x_rest(1, vbuf)
    x_near(2, qbuf)
    x_far(1, vbuf)
    sib_near(0, kbuf)
    sib_near(1, vbuf)
    forward(LEFT)
    forward(RIGHT)
    x_rest(2, qbuf)
    sib_far(0, kbuf)
    sib_far(1, vbuf)
    forward(DIAG)
    x_far(2, qbuf)

    y_wait(3, lambda s: ngbuf.at[s])
    for y in range(4):
        mixed = acc_m[y]
        centred = mixed - jnp.mean(mixed, axis=1, keepdims=True)
        inverse = lax.rsqrt(jnp.mean(centred * centred, axis=1, keepdims=True) + EPS)
        normed = centred * inverse
        nrmsrc[y] = normed.astype(BF16)
        ng = ngbuf[y]
        grad = ng - jnp.mean(ng, axis=1, keepdims=True)
        grad = (grad - normed * jnp.mean(ng * normed, axis=1, keepdims=True)) * inverse
        gbuf[y, xc] = grad.astype(BF16)
    x_start(3, gbuf)
    for y in range(4):
        send(nrmsrc.at[y], nrmbuf.at[yh], ret_sems.at[0, yh], (odp, y * 8 + xc))

    query_grads(0)
    x_near(3, gbuf)
    query_grads(LEFT)
    x_rest(3, gbuf)
    x_far(3, gbuf)
    query_grads(RIGHT)
    query_grads(DIAG)
    for y in range(4):
        out_q[y] = (acc_q[y] * 0.5).astype(BF16)
    give_back(1, out_q, dq_ref)

    rows = []
    for b in range(12):
        parts = []
        for at, d in enumerate(TABLED):
            low, high = spans[d]
            if low <= b <= high:
                got = acc_bias[at]
                dist = dist_q + 256 * d
                if b > low:
                    got = jnp.where(dist >= 2 ** (b - 1), got, 0.0)
                if b < high:
                    got = jnp.where(dist < 2**b, got, 0.0)
                parts.append(fold(got))
        if b == 10:
            parts.append(acc_far[0])
        if b == 11:
            parts += [acc_far[at] for at in range(1, 5)]
        whole = parts[0]
        for part in parts[1:]:
            whole = whole + part
        folded = jnp.sum(whole, axis=0, keepdims=True)
        rows.append(folded[:, :128] + folded[:, 128:])
    rows.append(jnp.zeros((4, 128), F32))
    shares = jnp.concatenate(rows, axis=0) * 0.5

    def share_out(stage, me, mine):
        red[stage, me] = mine
        for k in range(1, 8):
            dev, other = partners[stage](k)
            send(red.at[stage, me], red.at[stage, me], red_sems.at[stage, me], dev)

    def take_in(stage):
        for k in range(1, 8):
            other = partners[stage](k)[1]
            arrived(red.at[stage, other], red_sems.at[stage, other])

    def sum_of(stage):
        total = red[stage, 0]
        for k in range(1, 8):
            total = total + red[stage, k]
        return total

    share_out(0, z, shares)
    sib_own(2, qbuf)
    sib_own(3, gbuf)
    key_grads(0)
    take_in(0)
    share_out(1, xc, sum_of(0))
    sib_near(2, qbuf)
    sib_near(3, gbuf)
    key_grads(LEFT)
    key_grads(RIGHT)
    take_in(1)
    share_out(2, yi, sum_of(1))
    sib_far(2, qbuf)
    sib_far(3, gbuf)
    key_grads(DIAG)
    for y in range(4):
        out_v[y] = acc_v[y].astype(BF16)
        out_k[y] = (acc_k[y] * 0.5).astype(BF16)
    give_back(3, out_v, dv_ref)
    give_back(2, out_k, dk_ref)

    for h in range(4):
        arrived(nrmbuf.at[h], ret_sems.at[0, h])
        cols = slice(h * 128, (h + 1) * 128)
        gated_vm[:, cols] = (nrmbuf[h].astype(F32) * gates_vm[:, cols].astype(F32)).astype(BF16)
    outproj_vm[...] = dot_nn(gated_vm[...], proj_vm[...]).astype(BF16)
    out_copy = pltpu.make_async_copy(outproj_vm, projected_ref.at[0], local_sems.at[3])
    out_copy.start()

    take_in(2)
    by_head = lax.broadcasted_iota(jnp.int32, (16, 128), 0)
    by_lane = lax.broadcasted_iota(jnp.int32, (16, 128), 1)
    for h in range(4):
        sums = jnp.sum(red[2, h] + red[2, 4 + h], axis=1, keepdims=True)
        spread = jnp.where(by_head == by_lane, jnp.broadcast_to(sums, (16, 128)), 0.0)
        bias_ref[h : h + 1, :] = jnp.sum(spread, axis=0, keepdims=True)[:, :16]

    for a, out_ref in ((1, dq_ref), (3, dv_ref), (2, dk_ref)):
        for h in range(4):
            arrived(out_ref.at[0, :, h * 128 : (h + 1) * 128], ret_sems.at[a, h])
    out_copy.wait()
    for copy in pending:
        copy.wait_send()


def shards(queries, keys, values, gates, out_proj, out_grad, lengths, rel_bias):
    anywhere = pl.BlockSpec(memory_space=pl.ANY)
    scalars = pl.BlockSpec(memory_space=pltpu.SMEM)
    whole = pl.BlockSpec(memory_space=pltpu.VMEM)
    shape = jax.ShapeDtypeStruct
    head_rows = pltpu.VMEM((4, 8, 128, 128), BF16)
    own_rows = pltpu.VMEM((4, 128, 128), BF16)
    own_sums = pltpu.VMEM((4, 128, 128), F32)
    tables = pltpu.VMEM((4, 128, 256), F32)
    dma = pltpu.SemaphoreType.DMA
    return pl.pallas_call(
        kernel,
        out_shape=(
            shape((1, 128, 1024), BF16),
            shape((1, 128, 512), BF16),
            shape((1, 128, 512), BF16),
            shape((1, 128, 512), BF16),
            shape((4, 16), F32),
        ),
        in_specs=[anywhere] * 6 + [scalars] * 2,
        out_specs=(anywhere, anywhere, anywhere, anywhere, whole),
        scratch_shapes=[
            head_rows, head_rows, head_rows, head_rows,
            own_sums, own_sums, own_rows, own_rows,
            pltpu.VMEM((8, 128), F32), pltpu.VMEM((8, 128), F32),
            pltpu.VMEM((128, 1024), BF16),
            pltpu.VMEM((128, 512), BF16),
            pltpu.VMEM((512, 1024), BF16),
            pltpu.VMEM((128, 512), BF16),
            pltpu.VMEM((128, 1024), BF16),
            tables, tables, tables, tables,
            own_sums, own_sums, own_sums, own_sums,
            own_rows, own_rows, own_rows,
            tables, pltpu.VMEM((5, 8, 256), F32),
            pltpu.VMEM((3, 8, 16, 128), F32),
            dma((112,)), dma((4, 4)), dma((4, 13)), dma((4, 4)), dma((3, 8)), dma((1,)), dma((4,)),
        ],
        compiler_params=pltpu.CompilerParams(
            collective_id=0, has_side_effects=True, vmem_limit_bytes=48 * 2**20
        ),
    )(queries, keys, values, gates, out_proj, out_grad, lengths, rel_bias)


def solution(mesh):
    rows = P("dp", "seq", None)
    return jax.shard_map(
        shards,
        mesh=mesh,
        in_specs=(rows, rows, rows, rows, P(), rows, P("dp", None), P()),
        out_specs=(rows, rows, rows, rows, P()),
        check_vma=False,
    )
```

time: 504 us -> 79.2 us (0.16)
  waiting for transfers between devices: 184 us -> 0 us
  blocking collectives: 119 us -> 0 us
  local copies, waits for them, and re-layouts: 98.5 us -> 10.4 us
  Pallas kernels: 0 us -> 67.8 us
  matrix products: 41.5 us -> 0 us
  loops' own time: 30.6 us -> 0 us
  between operations: 14 us -> 0.66 us
  other arithmetic: 12.4 us -> 0 us
    all_gather x4 -> x0, waiting for transfers between devices: 184 us -> none  [the longest x1 68.8 us: shards(): lax.all_gather(own_keys, 'seq', axis=0, tiled=True)]
    psum x1 -> x0, blocking collectives: 119 us -> none  [shards(): bias_grad = lax.psum(bias_part, ('dp', 'seq'))]
    pallas_call x0 -> x1, Pallas kernels: none -> 67.8 us  [shards(): pl.pallas_call(kernel, out_shape=(shape((1, 128, 1024), BF16), shape((1,...]
    unnamed x28 -> x21, local copies, waits for them, and re-layouts: 56.2 us -> 10.4 us
    dot_general x25 -> x0, matrix products: 41.5 us -> none  [the longest x3 8.61 us: key_step(): jnp.einsum('hqk,qkb->hb', score_grad, one_hot, precision=lax.Precision.HI...]
    another operation x27 -> x0, loops' own time: 30.6 us -> none  [the longest x3 29.9 us: over_blocks(): lax.scan(advance, running, (jnp.arange(block_count, dtype=jnp.int32), sta...]
    dynamic_slice x24 -> x0, local copies, waits for them, and re-layouts: 24.9 us -> none  [over_blocks(): lax.scan(advance, running, (jnp.arange(block_count, dtype=jnp.int32), sta...]
    all_gather x1 -> x0, local copies, waits for them, and re-layouts: 6.35 us -> none  [shards(): query_piece = lax.all_gather(own_queries, 'seq', axis=0, tiled=True)]
  transfers between devices with their start and end apart: 4 -> 0, of which waited for: 3 -> 0; matrix products, arithmetic and copies ran while one was open for 19% -> 0% of each run, Pallas kernels for 0% -> 0%
where the time goes in v1:
time: 79.2 us; the launch traced here: 78.8 us
  Pallas kernels  67.8 us (86%)
  local copies, waits for them, and re-layouts  10.4 us (13%)
    pallas_call x1, Pallas kernels, shards(): pl.pallas_call(kernel, out_shape=(shape((1, 128, 1024), BF16), shape((1,...  67.8 us
    unnamed x21, local copies, waits for them, and re-layouts  10.4 us

profile of v1, /device:TPU:1, one launch (start us, length us, event | category | flops | bytes accessed | tf_op | source)
XLA Modules:
  0.0 78.8 jit_solution(13376559965166001776)
XLA Ops:
  0.6 0.0 copy-start
  0.6 1.2 %copy-done = bf16[512,1024]{1,0:T(8,128)(2,1)S(1)} copy-done((bf16[512,1024]{1,0:T(8,128)(2,1)S(1)}, bf16[512,1024]{1,0:T(8,128)(2,1)}, u32[]{:S(2)}) %copy-start) | copy-done | bytes 1048600
  1.9 0.0 copy-start.1
  1.9 0.9 %copy-done.1 = bf16[1,128,1024]{2,1,0:T(8,128)(2,1)S(1)} copy-done((bf16[1,128,1024]{2,1,0:T(8,128)(2,1)S(1)}, bf16[1,128,1024]{2,1,0:T(8,128)(2,1)}, u32[]{:S(2)}) %copy-start.1) | copy-done | bytes 262168
  2.8 0.0 copy-start.2
  2.8 0.9 %copy-done.2 = bf16[1,128,512]{2,1,0:T(8,128)(2,1)S(1)} copy-done((bf16[1,128,512]{2,1,0:T(8,128)(2,1)S(1)}, bf16[1,128,512]{2,1,0:T(8,128)(2,1)}, u32[]{:S(2)}) %copy-start.2) | copy-done | bytes 131096
  3.7 0.0 copy-start.3
  3.7 0.9 %copy-done.3 = bf16[1,128,512]{2,1,0:T(8,128)(2,1)S(1)} copy-done((bf16[1,128,512]{2,1,0:T(8,128)(2,1)S(1)}, bf16[1,128,512]{2,1,0:T(8,128)(2,1)}, u32[]{:S(2)}) %copy-start.3) | copy-done | bytes 131096
  4.6 0.0 copy-start.4
  4.6 0.9 %copy-done.4 = bf16[1,128,512]{2,1,0:T(8,128)(2,1)S(1)} copy-done((bf16[1,128,512]{2,1,0:T(8,128)(2,1)S(1)}, bf16[1,128,512]{2,1,0:T(8,128)(2,1)}, u32[]{:S(2)}) %copy-start.4) | copy-done | bytes 131096
  5.5 0.0 copy-start.5
  5.5 0.9 %copy-done.5 = bf16[1,128,512]{2,1,0:T(8,128)(2,1)S(1)} copy-done((bf16[1,128,512]{2,1,0:T(8,128)(2,1)S(1)}, bf16[1,128,512]{2,1,0:T(8,128)(2,1)}, u32[]{:S(2)}) %copy-start.5) | copy-done | bytes 131096
  6.4 0.0 copy-start.6
  6.4 0.7 copy-done.6
  7.1 0.0 copy-start.7
  7.1 0.7 copy-done.7
  7.8 67.8 %shard_map.119 = (bf16[1,128,1024]{2,1,0:T(8,128)(2,1)S(1)}, bf16[1,128,512]{2,1,0:T(8,128)(2,1)S(1)}, bf16[1,128,512]{2,1,0:T(8,128)(2,1)S(1)}, bf16[1,128,512]{2,1,0:T(8,128)(2,1)S(1)}, f32[4,16]{1,0:T(4,128)S(1)}) custom-call(bf16[1,128,512]{2,1,0:T(8,128)(2,1)S(1)} %copy-done.2, bf16[1,128,512]{2,1,0:T(8,128)(2,1)S(1)} %copy-done.3, ...), custom_call_target="tpu_custom_call" | custom-call | tf_op jit(solution)/shard_map/pallas_call | solution.py:472
  75.6 0.7 copy.18
  76.3 0.7 copy.19
  76.9 0.7 copy.20
  77.6 0.7 copy.21
  78.3 0.6 copy.22
Async XLA Ops:
  0.6 1.2 %copy-start = (bf16[512,1024]{1,0:T(8,128)(2,1)S(1)}, bf16[512,1024]{1,0:T(8,128)(2,1)}, u32[]{:S(2)}) copy-start(bf16[512,1024]{1,0:T(8,128)(2,1)} %proj_in.1) | copy-start | bytes 3145732
  1.9 0.9 %copy-start.1 = (bf16[1,128,1024]{2,1,0:T(8,128)(2,1)S(1)}, bf16[1,128,1024]{2,1,0:T(8,128)(2,1)}, u32[]{:S(2)}) copy-start(bf16[1,128,1024]{2,1,0:T(8,128)(2,1)} %og_in.1) | copy-start | bytes 786436
  2.8 0.9 %copy-start.2 = (bf16[1,128,512]{2,1,0:T(8,128)(2,1)S(1)}, bf16[1,128,512]{2,1,0:T(8,128)(2,1)}, u32[]{:S(2)}) copy-start(bf16[1,128,512]{2,1,0:T(8,128)(2,1)} %q_in.1) | copy-start | bytes 393220
  3.7 0.9 %copy-start.3 = (bf16[1,128,512]{2,1,0:T(8,128)(2,1)S(1)}, bf16[1,128,512]{2,1,0:T(8,128)(2,1)}, u32[]{:S(2)}) copy-start(bf16[1,128,512]{2,1,0:T(8,128)(2,1)} %k_in.1) | copy-start | bytes 393220
  4.6 0.9 %copy-start.4 = (bf16[1,128,512]{2,1,0:T(8,128)(2,1)S(1)}, bf16[1,128,512]{2,1,0:T(8,128)(2,1)}, u32[]{:S(2)}) copy-start(bf16[1,128,512]{2,1,0:T(8,128)(2,1)} %v_in.1) | copy-start | bytes 393220
  5.5 0.9 %copy-start.5 = (bf16[1,128,512]{2,1,0:T(8,128)(2,1)S(1)}, bf16[1,128,512]{2,1,0:T(8,128)(2,1)}, u32[]{:S(2)}) copy-start(bf16[1,128,512]{2,1,0:T(8,128)(2,1)} %gates_in.1) | copy-start | bytes 393220
  6.4 0.7 copy-start.6
  7.1 0.7 copy-start.7

commit v2 on v1

--- a/solution.py
+++ b/solution.py
@@ -24,12 +24,13 @@
 
 
 def kernel(
-    q_in, k_in, v_in, gates_in, proj_in, og_in, len_ref, rb_ref,
+    q_in, k_in, v_in, gates_in, proj_in, og_in, len_in, rb_in,
     projected_ref, dq_ref, dk_ref, dv_ref, bias_ref,
     kbuf, vbuf, qbuf, gbuf, ngbuf, ngsrc, nrmsrc, nrmbuf, lensrc, lenbuf,
     og_vm, gates_vm, proj_vm, gated_vm, outproj_vm,
-    tab_q, tab_k, st_t, en_t, acc_m, acc_q, acc_k, acc_v,
+    slopes, tab_b, tab_q, tab_k, st_t, en_t, acc_m, acc_q, acc_k, acc_v,
     out_q, out_k, out_v, acc_bias, acc_far, red,
+    len_ref, rb_ref,
     send_sems, y_sems, x_sems, ret_sems, red_sems, len_sem, local_sems,
 ):
     dp = lax.axis_index("dp")
@@ -60,31 +61,39 @@
         other = lax.rem(yi + k, 8)
         return (lax.div(other, 4) * 8 + z, lax.rem(other, 4) * 8 + xc), other
 
-    partners = (z_partner, xc_partner, y_partner)
+    partners = (y_partner, xc_partner, z_partner)
 
     barrier = pltpu.get_barrier_semaphore()
-    for partner in (y_partner, xc_partner, z_partner):
+
+    def greet(dev):
+        pl.semaphore_signal(barrier, inc=1, device_id=dev, device_id_type=pl.DeviceIdType.MESH)
+
+    def group_of(plane):
+        return plane - lax.div(plane, 4) * lax.rem(plane, 4)
+
+    def greet_planes(same):
         for k in range(1, 8):
-            pl.semaphore_signal(
-                barrier, inc=1, device_id=partner(k)[0], device_id_type=pl.DeviceIdType.MESH
-            )
+            dev, other = z_partner(k)
+            meets = group_of(other) == group_of(z)
+            pl.when(meets if same else jnp.logical_not(meets))(lambda dev=dev: greet(dev))
+
+    for partner in (y_partner, xc_partner):
+        for k in range(1, 8):
+            greet(partner(k)[0])
+    greet_planes(True)
+    earlier = z + lax.div(z, 4) * (7 - z)
 
     local = [
         pltpu.make_async_copy(og_in.at[0], og_vm, local_sems.at[0]),
         pltpu.make_async_copy(proj_in, proj_vm, local_sems.at[1]),
         pltpu.make_async_copy(gates_in.at[0], gates_vm, local_sems.at[2]),
     ]
-    ends = []
-    total = len_ref[0, 0]
-    ends.append(total)
-    for u in range(1, 4):
-        total = total + len_ref[0, u]
-        ends.append(total)
-    row_at = lax.broadcasted_iota(jnp.int32, (8, 128), 0)
-    end_rows = jnp.zeros((8, 128), F32)
-    for u in range(4):
-        end_rows = jnp.where(row_at == u, ends[u].astype(F32), end_rows)
-    lensrc[...] = end_rows
+    small = [
+        pltpu.make_async_copy(len_in, len_ref, local_sems.at[4]),
+        pltpu.make_async_copy(rb_in, rb_ref, local_sems.at[5]),
+    ]
+    for copy in small + local:
+        copy.start()
 
     pending = []
 
@@ -99,7 +108,7 @@
     def arrived(dst, sem):
         pltpu.make_async_copy(dst, dst, sem).wait()
 
-    pl.semaphore_wait(barrier, 21)
+    pl.semaphore_wait(barrier, 14 + earlier)
 
     def y_send(a, src_of, dst):
         for h in range(4):
@@ -111,10 +120,18 @@
 
     for a, (src, buf) in enumerate(((k_in, kbuf), (v_in, vbuf), (q_in, qbuf))):
         y_send(a, lambda h, src=src: src.at[0, :, h * 128 : (h + 1) * 128], buf.at[yh, xc])
-        if a == 0:
-            send(lensrc, lenbuf, len_sem.at[0], (odp, seq))
-    for copy in local:
-        copy.start()
+    greet_planes(False)
+    for copy in small:
+        copy.wait()
+    ends = [len_ref[0, 0]]
+    for u in range(1, 4):
+        ends.append(ends[-1] + len_ref[0, u])
+    row_at = lax.broadcasted_iota(jnp.int32, (8, 128), 0)
+    end_rows = jnp.zeros((8, 128), F32)
+    for u in range(4):
+        end_rows = jnp.where(row_at == u, ends[u].astype(F32), end_rows)
+    lensrc[...] = end_rows
+    send(lensrc, lenbuf, len_sem.at[0], (odp, seq))
 
     def piece(buf, half, at):
         return buf.at[pl.ds(2 * half, 2), at]
@@ -122,13 +139,20 @@
     def own_of(at):
         return at * 2 + c
 
+    def x_half(a, buf, half):
+        part = piece(buf, half, own_of(x))
+        if half == 0:
+            send(part, part, x_sems.at[a, 0], dev_right)
+            send(part, part, x_sems.at[a, 4], dev_left)
+            send(part, part, x_sems.at[a, 6], dev_sib)
+        else:
+            send(part, part, x_sems.at[a, 3], dev_left)
+            send(part, part, x_sems.at[a, 1], dev_right)
+            send(part, part, x_sems.at[a, 13], dev_sib)
+
     def x_start(a, buf):
-        mine = own_of(x)
-        send(piece(buf, 0, mine), piece(buf, 0, mine), x_sems.at[a, 0], dev_right)
-        send(piece(buf, 1, mine), piece(buf, 1, mine), x_sems.at[a, 3], dev_left)
-        send(piece(buf, 1, mine), piece(buf, 1, mine), x_sems.at[a, 1], dev_right)
-        send(piece(buf, 0, mine), piece(buf, 0, mine), x_sems.at[a, 4], dev_left)
-        send(buf.at[:, mine], buf.at[:, mine], x_sems.at[a, 6], dev_sib)
+        x_half(a, buf, 0)
+        x_half(a, buf, 1)
 
     def x_pass(a, buf, steps):
         for half, whose, slot, to in steps:
@@ -152,7 +176,8 @@
         return at * 2 + 1 - c
 
     def sib_own(a, buf):
-        arrived(buf.at[:, sib_of(x)], x_sems.at[a, 6])
+        arrived(piece(buf, 0, sib_of(x)), x_sems.at[a, 6])
+        arrived(piece(buf, 1, sib_of(x)), x_sems.at[a, 13])
 
     def sib_near(a, buf):
         arrived(piece(buf, 0, sib_of(left)), x_sems.at[a, 7])
@@ -171,10 +196,10 @@
     dist_k = lane - sub - 128 * c
     half_bias = [0.5 * rb_ref[yh, b] for b in range(12)]
 
-    def biases(dist, low, high):
-        filled = jnp.full(wide, half_bias[low], F32)
+    def biases(dist, low, high, values):
+        filled = jnp.full(wide, values[low], F32)
         for b in range(low + 1, high + 1):
-            filled = jnp.where(dist >= 2 ** (b - 1), half_bias[b], filled)
+            filled = jnp.where(dist >= 2 ** (b - 1), values[b], filled)
         return filled
 
     spans = {0: (0, 9), 1: (1, 9), 2: (9, 10), 4: (10, 11)}
@@ -182,10 +207,12 @@
     def build_tables():
         for tab, dist in ((tab_q, dist_q), (tab_k, dist_k)):
             for at, d in enumerate(TABLED):
-                filled = biases(dist + 256 * d, *spans[d])
+                filled = biases(dist + 256 * d, *spans[d], half_bias)
                 if d == 0:
                     filled = jnp.where(dist >= 0, filled, NEG)
                 tab[at] = filled
+        for at, d in enumerate(TABLED):
+            tab_b[at] = biases(dist_q + 256 * d, *spans[d], [float(b) for b in range(12)])
 
     def bias_at(tab, d):
         if d in TABLED:
@@ -219,10 +246,10 @@
     def pair(buf, y, at):
         return buf[y, pl.ds(at * 2, 2)].reshape(256, 128)
 
-    def query_tiles(r):
+    def query_tiles(r, ys):
         at = lax.rem(x - r + 4, 4)
         wrap = 1 - lax.div(x - r + 4, 4)
-        for y in range(4):
+        for y in ys:
             tiles = []
             for j in range(3 if r == 0 else 2):
                 if y < j:
@@ -235,10 +262,10 @@
                 tiles.append((r + 4 * j, ky, first))
             yield y, at, tiles
 
-    def key_tiles(r):
+    def key_tiles(r, ys):
         at = lax.rem(x + r, 4)
         wrap = lax.div(x + r, 4)
-        for y in range(4):
+        for y in ys:
             tiles = []
             for j in range(3 if r == 0 else 2):
                 if y + j > 3:
@@ -251,32 +278,33 @@
                 tiles.append((r + 4 * j, qy, first))
             yield y, at, tiles
 
-    def forward(r):
-        for y, at, tiles in query_tiles(r):
+    def slot_of(y, d):
+        return (0, 4, 12, 21)[y] + d
+
+    def forward(r, ys=range(4)):
+        for y, at, tiles in query_tiles(r, ys):
             part = None if r == 0 else acc_m[y]
             for d, ky, first in tiles:
                 s = dot_nt(qbuf[y, xc], pair(kbuf, ky, at))
                 t = s * HALF_SCALE + bias_at(tab_q, d)
                 t = jnp.where(st_t[y] <= first, t, NEG)
-                w = (t * jnp.tanh(t) + t).astype(BF16)
-                add = dot_nn(w, pair(vbuf, ky, at))
+                th = jnp.tanh(t)
+                one = 1.0 + th
+                slopes[slot_of(y, d)] = one * (1.0 + t * (1.0 - th))
+                add = dot_nn((t * one).astype(BF16), pair(vbuf, ky, at))
                 part = add if part is None else part + add
             acc_m[y] = part
 
     def fold(ds):
         return jnp.sum(ds.reshape(16, 8, 256), axis=0)
 
-    def query_grads(r):
+    def query_grads(r, ys=range(4)):
         sums = {}
-        for y, at, tiles in query_tiles(r):
+        for y, at, tiles in query_tiles(r, ys):
             part = None if r == 0 else acc_q[y]
             for d, ky, first in tiles:
                 keys = pair(kbuf, ky, at)
-                s = dot_nt(qbuf[y, xc], keys)
-                t = s * HALF_SCALE + bias_at(tab_q, d)
-                t = jnp.where(st_t[y] <= first, t, NEG)
-                th = jnp.tanh(t)
-                ds = dot_nt(gbuf[y, xc], pair(vbuf, ky, at)) * ((1.0 + th) * (1.0 + t * (1.0 - th)))
+                ds = dot_nt(gbuf[y, xc], pair(vbuf, ky, at)) * slopes[slot_of(y, d)]
                 if d in TABLED:
                     slot = acc_bias.at[TABLED.index(d)]
                     slot[...] = ds if d not in sums else slot[...] + ds
@@ -288,8 +316,8 @@
                 part = add if part is None else part + add
             acc_q[y] = part
 
-    def key_grads(r):
-        for y, at, tiles in key_tiles(r):
+    def key_grads(r, ys=range(4)):
+        for y, at, tiles in key_tiles(r, ys):
             key_part = None if r == 0 else acc_k[y]
             value_part = None if r == 0 else acc_v[y]
             for d, qy, first in tiles:
@@ -311,8 +339,8 @@
     def own_cols(h):
         return pl.ds(pl.multiple_of(h * 128, 128), 128)
 
-    def give_back(a, src, out_ref):
-        for y in range(4):
+    def give_back(a, src, out_ref, ys=range(4)):
+        for y in ys:
             send(
                 src.at[y], out_ref.at[0, :, own_cols(yh)], ret_sems.at[a, yh], (odp, y * 8 + xc)
             )
@@ -322,32 +350,30 @@
     gate_grads()
     y_wait(1, lambda s: vbuf.at[s, xc])
     x_start(1, vbuf)
+    build_tables()
     x_near(0, kbuf)
-    build_tables()
     x_rest(0, kbuf)
     y_wait(2, lambda s: qbuf.at[s, xc])
+    build_bounds()
+    x_near(1, vbuf)
     x_start(2, qbuf)
-    x_near(1, vbuf)
-    x_far(0, kbuf)
-    build_bounds()
     sib_own(0, kbuf)
     sib_own(1, vbuf)
     forward(0)
+    x_far(0, kbuf)
     x_rest(1, vbuf)
-    x_near(2, qbuf)
-    x_far(1, vbuf)
     sib_near(0, kbuf)
     sib_near(1, vbuf)
     forward(LEFT)
+    x_far(1, vbuf)
+    x_near(2, qbuf)
     forward(RIGHT)
     x_rest(2, qbuf)
     sib_far(0, kbuf)
     sib_far(1, vbuf)
-    forward(DIAG)
-    x_far(2, qbuf)
-
     y_wait(3, lambda s: ngbuf.at[s])
-    for y in range(4):
+
+    def finish(y):
         mixed = acc_m[y]
         centred = mixed - jnp.mean(mixed, axis=1, keepdims=True)
         inverse = lax.rsqrt(jnp.mean(centred * centred, axis=1, keepdims=True) + EPS)
@@ -357,34 +383,29 @@
         grad = ng - jnp.mean(ng, axis=1, keepdims=True)
         grad = (grad - normed * jnp.mean(ng * normed, axis=1, keepdims=True)) * inverse
         gbuf[y, xc] = grad.astype(BF16)
-    x_start(3, gbuf)
+
+    for half in range(2):
+        ys = (2 * half, 2 * half + 1)
+        forward(DIAG, ys)
+        for y in ys:
+            finish(y)
+        x_half(3, gbuf, half)
     for y in range(4):
         send(nrmsrc.at[y], nrmbuf.at[yh], ret_sems.at[0, yh], (odp, y * 8 + xc))
+    x_far(2, qbuf)
 
     query_grads(0)
+    query_grads(LEFT)
+    query_grads(RIGHT)
     x_near(3, gbuf)
-    query_grads(LEFT)
-    x_rest(3, gbuf)
-    x_far(3, gbuf)
-    query_grads(RIGHT)
     query_grads(DIAG)
-    for y in range(4):
-        out_q[y] = (acc_q[y] * 0.5).astype(BF16)
-    give_back(1, out_q, dq_ref)
-
     rows = []
     for b in range(12):
         parts = []
         for at, d in enumerate(TABLED):
             low, high = spans[d]
             if low <= b <= high:
-                got = acc_bias[at]
-                dist = dist_q + 256 * d
-                if b > low:
-                    got = jnp.where(dist >= 2 ** (b - 1), got, 0.0)
-                if b < high:
-                    got = jnp.where(dist < 2**b, got, 0.0)
-                parts.append(fold(got))
+                parts.append(fold(jnp.where(tab_b[at] == float(b), acc_bias[at], 0.0)))
         if b == 10:
             parts.append(acc_far[0])
         if b == 11:
@@ -414,26 +435,44 @@
             total = total + red[stage, k]
         return total
 
-    share_out(0, z, shares)
+    by_head = lax.broadcasted_iota(jnp.int32, (16, 128), 0)
+    by_lane = lax.broadcasted_iota(jnp.int32, (16, 128), 1)
+
+    def heads_side_by_side():
+        packed = jnp.zeros((16, 128), F32)
+        for h in range(4):
+            sums = jnp.sum(red[0, h] + red[0, 4 + h], axis=1, keepdims=True)
+            packed = jnp.where(by_lane == h, jnp.broadcast_to(sums, (16, 128)), packed)
+        return packed
+
+    pl.when(z < 4)(lambda: pl.semaphore_wait(barrier, 7 - earlier))
+    share_out(0, yi, shares)
+    x_rest(3, gbuf)
+    for y in range(4):
+        out_q[y] = (acc_q[y] * 0.5).astype(BF16)
+    give_back(1, out_q, dq_ref)
     sib_own(2, qbuf)
     sib_own(3, gbuf)
     key_grads(0)
+    x_far(3, gbuf)
     take_in(0)
-    share_out(1, xc, sum_of(0))
+    share_out(1, xc, heads_side_by_side())
     sib_near(2, qbuf)
     sib_near(3, gbuf)
     key_grads(LEFT)
+    take_in(1)
+    share_out(2, z, sum_of(1))
     key_grads(RIGHT)
-    take_in(1)
-    share_out(2, yi, sum_of(1))
     sib_far(2, qbuf)
     sib_far(3, gbuf)
-    key_grads(DIAG)
-    for y in range(4):
-        out_v[y] = acc_v[y].astype(BF16)
-        out_k[y] = (acc_k[y] * 0.5).astype(BF16)
-    give_back(3, out_v, dv_ref)
-    give_back(2, out_k, dk_ref)
+    for half in range(2):
+        ys = (2 * half, 2 * half + 1)
+        key_grads(DIAG, ys)
+        for y in ys:
+            out_v[y] = acc_v[y].astype(BF16)
+            out_k[y] = (acc_k[y] * 0.5).astype(BF16)
+        give_back(3, out_v, dv_ref, ys)
+        give_back(2, out_k, dk_ref, ys)
 
     for h in range(4):
         arrived(nrmbuf.at[h], ret_sems.at[0, h])
@@ -444,10 +483,9 @@
     out_copy.start()
 
     take_in(2)
-    by_head = lax.broadcasted_iota(jnp.int32, (16, 128), 0)
-    by_lane = lax.broadcasted_iota(jnp.int32, (16, 128), 1)
+    heads = sum_of(2)
     for h in range(4):
-        sums = jnp.sum(red[2, h] + red[2, 4 + h], axis=1, keepdims=True)
+        sums = jnp.sum(jnp.where(by_lane == h, heads, 0.0), axis=1, keepdims=True)
         spread = jnp.where(by_head == by_lane, jnp.broadcast_to(sums, (16, 128)), 0.0)
         bias_ref[h : h + 1, :] = jnp.sum(spread, axis=0, keepdims=True)[:, :16]
 
@@ -459,9 +497,13 @@
         copy.wait_send()
 
 
+def hand_out(*refs):
+    for i in range(5):
+        refs[5 + i][...] = refs[i][...]
+
+
 def shards(queries, keys, values, gates, out_proj, out_grad, lengths, rel_bias):
     anywhere = pl.BlockSpec(memory_space=pl.ANY)
-    scalars = pl.BlockSpec(memory_space=pltpu.SMEM)
     whole = pl.BlockSpec(memory_space=pltpu.VMEM)
     shape = jax.ShapeDtypeStruct
     head_rows = pltpu.VMEM((4, 8, 128, 128), BF16)
@@ -469,16 +511,17 @@
     own_sums = pltpu.VMEM((4, 128, 128), F32)
     tables = pltpu.VMEM((4, 128, 256), F32)
     dma = pltpu.SemaphoreType.DMA
-    return pl.pallas_call(
-        kernel,
-        out_shape=(
+    made = (
             shape((1, 128, 1024), BF16),
             shape((1, 128, 512), BF16),
             shape((1, 128, 512), BF16),
             shape((1, 128, 512), BF16),
             shape((4, 16), F32),
-        ),
-        in_specs=[anywhere] * 6 + [scalars] * 2,
+        )
+    results = pl.pallas_call(
+        kernel,
+        out_shape=made,
+        in_specs=[anywhere] * 8,
         out_specs=(anywhere, anywhere, anywhere, anywhere, whole),
         scratch_shapes=[
             head_rows, head_rows, head_rows, head_rows,
@@ -489,17 +532,25 @@
             pltpu.VMEM((512, 1024), BF16),
             pltpu.VMEM((128, 512), BF16),
             pltpu.VMEM((128, 1024), BF16),
+            pltpu.VMEM((30, 128, 256), F32), pltpu.VMEM((4, 128, 256), F32),
             tables, tables, tables, tables,
             own_sums, own_sums, own_sums, own_sums,
             own_rows, own_rows, own_rows,
             tables, pltpu.VMEM((5, 8, 256), F32),
             pltpu.VMEM((3, 8, 16, 128), F32),
-            dma((112,)), dma((4, 4)), dma((4, 13)), dma((4, 4)), dma((3, 8)), dma((1,)), dma((4,)),
+            pltpu.SMEM((1, 4), jnp.int32), pltpu.SMEM((4, 16), F32),
+            dma((116,)), dma((4, 4)), dma((4, 14)), dma((4, 4)), dma((3, 8)), dma((1,)), dma((6,)),
         ],
         compiler_params=pltpu.CompilerParams(
-            collective_id=0, has_side_effects=True, vmem_limit_bytes=48 * 2**20
+            collective_id=0, has_side_effects=True, vmem_limit_bytes=60 * 2**20
         ),
     )(queries, keys, values, gates, out_proj, out_grad, lengths, rel_bias)
+    return pl.pallas_call(
+        hand_out,
+        out_shape=made,
+        in_specs=[whole] * 5,
+        out_specs=(whole,) * 5,
+    )(*results)
 
 
 def solution(mesh):

time: 79.2 us -> 60.5 us (0.76)
  local copies, waits for them, and re-layouts: 10.4 us -> 0 us
  Pallas kernels: 67.8 us -> 59.7 us
    unnamed x21 -> x0, local copies, waits for them, and re-layouts: 10.4 us -> none
    pallas_call x1 -> x2, Pallas kernels: 67.8 us -> 59.7 us  [the longest x1 57.8 us: shards(): pl.pallas_call(kernel, out_shape=made, in_specs=[anywhere] * 8, out_specs...]
where the time goes in v2:
time: 60.5 us; the launch traced here: 60.4 us
  Pallas kernels  59.7 us (99%)
  between operations  0.64 us (1%)
    pallas_call x1, Pallas kernels, shards(): pl.pallas_call(kernel, out_shape=made, in_specs=[anywhere] * 8, out_specs...  57.8 us
    pallas_call x1, Pallas kernels, shards(): pl.pallas_call(hand_out, out_shape=made, in_specs=[whole] * 5, out_specs=...  1.96 us

profile of v2, /device:TPU:1, one launch (start us, length us, event | category | flops | bytes accessed | tf_op | source)
XLA Modules:
  0.0 60.4 jit_solution(15640917359886483101)
XLA Ops:
  0.6 57.8 %shard_map.119 = (bf16[1,128,1024]{2,1,0:T(8,128)(2,1)}, bf16[1,128,512]{2,1,0:T(8,128)(2,1)}, bf16[1,128,512]{2,1,0:T(8,128)(2,1)}, bf16[1,128,512]{2,1,0:T(8,128)(2,1)}, f32[4,16]{1,0:T(4,128)}) custom-call(bf16[1,128,512]{2,1,0:T(8,128)(2,1)} %q_in.1, bf16[1,128,512]{2,1,0:T(8,128)(2,1)} %k_in.1, bf16[1,128,512]{2,1,0:T(8,128)(2,1)} %v_in.1, ...), custom_call_target="tpu_custom_call" | custom-call | tf_op jit(solution)/shard_map/pallas_call | solution.py:521
  58.4 2.0 %shard_map.120 = (bf16[1,128,1024]{2,1,0:T(8,128)(2,1)}, bf16[1,128,512]{2,1,0:T(8,128)(2,1)}, bf16[1,128,512]{2,1,0:T(8,128)(2,1)}, bf16[1,128,512]{2,1,0:T(8,128)(2,1)}, f32[4,16]{1,0:T(4,128)}) custom-call(bf16[1,128,1024]{2,1,0:T(8,128)(2,1)} %get-tuple-element.10.refs_0_, bf16[1,128,512]{2,1,0:T(8,128)(2,1)} %get-tuple-element.11.refs_1_, ...), custom_call_target="tpu_custom_call" | custom-call | tf_op jit(solution)/shard_map/pallas_call | solution.py:548

commit v3 on v2

--- a/solution.py
+++ b/solution.py
@@ -416,7 +416,11 @@
         folded = jnp.sum(whole, axis=0, keepdims=True)
         rows.append(folded[:, :128] + folded[:, 128:])
     rows.append(jnp.zeros((4, 128), F32))
-    shares = jnp.concatenate(rows, axis=0) * 0.5
+    shares = jnp.sum(jnp.concatenate(rows, axis=0), axis=1, keepdims=True) * 0.5
+    by_bucket = lax.broadcasted_iota(jnp.int32, (16, 128), 0)
+    by_lane = lax.broadcasted_iota(jnp.int32, (16, 128), 1)
+    shares = jnp.where(by_lane == by_bucket + 16 * yh, jnp.broadcast_to(shares, (16, 128)), 0.0)
+    shares = jnp.sum(shares, axis=0, keepdims=True)
 
     def share_out(stage, me, mine):
         red[stage, me] = mine
@@ -434,16 +438,6 @@
         for k in range(1, 8):
             total = total + red[stage, k]
         return total
-
-    by_head = lax.broadcasted_iota(jnp.int32, (16, 128), 0)
-    by_lane = lax.broadcasted_iota(jnp.int32, (16, 128), 1)
-
-    def heads_side_by_side():
-        packed = jnp.zeros((16, 128), F32)
-        for h in range(4):
-            sums = jnp.sum(red[0, h] + red[0, 4 + h], axis=1, keepdims=True)
-            packed = jnp.where(by_lane == h, jnp.broadcast_to(sums, (16, 128)), packed)
-        return packed
 
     pl.when(z < 4)(lambda: pl.semaphore_wait(barrier, 7 - earlier))
     share_out(0, yi, shares)
@@ -455,13 +449,11 @@
     sib_own(3, gbuf)
     key_grads(0)
     x_far(3, gbuf)
-    take_in(0)
-    share_out(1, xc, heads_side_by_side())
     sib_near(2, qbuf)
     sib_near(3, gbuf)
     key_grads(LEFT)
-    take_in(1)
-    share_out(2, z, sum_of(1))
+    take_in(0)
+    share_out(1, xc, sum_of(0))
     key_grads(RIGHT)
     sib_far(2, qbuf)
     sib_far(3, gbuf)
@@ -474,6 +466,9 @@
         give_back(3, out_v, dv_ref, ys)
         give_back(2, out_k, dk_ref, ys)
 
+    take_in(1)
+    share_out(2, z, sum_of(1))
+
     for h in range(4):
         arrived(nrmbuf.at[h], ret_sems.at[0, h])
         cols = slice(h * 128, (h + 1) * 128)
@@ -483,11 +478,9 @@
     out_copy.start()
 
     take_in(2)
-    heads = sum_of(2)
+    sums = sum_of(2)
     for h in range(4):
-        sums = jnp.sum(jnp.where(by_lane == h, heads, 0.0), axis=1, keepdims=True)
-        spread = jnp.where(by_head == by_lane, jnp.broadcast_to(sums, (16, 128)), 0.0)
-        bias_ref[h : h + 1, :] = jnp.sum(spread, axis=0, keepdims=True)[:, :16]
+        bias_ref[h : h + 1, :] = sums[:, 16 * h : 16 * h + 16]
 
     for a, out_ref in ((1, dq_ref), (3, dv_ref), (2, dk_ref)):
         for h in range(4):
@@ -537,7 +530,7 @@
             own_sums, own_sums, own_sums, own_sums,
             own_rows, own_rows, own_rows,
             tables, pltpu.VMEM((5, 8, 256), F32),
-            pltpu.VMEM((3, 8, 16, 128), F32),
+            pltpu.VMEM((3, 8, 1, 128), F32),
             pltpu.SMEM((1, 4), jnp.int32), pltpu.SMEM((4, 16), F32),
             dma((116,)), dma((4, 4)), dma((4, 14)), dma((4, 4)), dma((3, 8)), dma((1,)), dma((6,)),
         ],

time: 60.5 us -> 58.5 us (0.967)
  Pallas kernels: 59.7 us -> 57.7 us
    pallas_call x1, Pallas kernels: 57.8 us -> 55.8 us  [shards(): pl.pallas_call(kernel, out_shape=made, in_specs=[anywhere] * 8, out_specs...]
where the time goes in v3:
time: 58.5 us; the launch traced here: 58.4 us
  Pallas kernels  57.7 us (99%)
  between operations  0.64 us (1%)
    pallas_call x1, Pallas kernels, shards(): pl.pallas_call(kernel, out_shape=made, in_specs=[anywhere] * 8, out_specs...  55.8 us
    pallas_call x1, Pallas kernels, shards(): pl.pallas_call(hand_out, out_shape=made, in_specs=[whole] * 5, out_specs=...  1.96 us

profile of v3, /device:TPU:1, one launch (start us, length us, event | category | flops | bytes accessed | tf_op | source)
XLA Modules:
  0.0 58.4 jit_solution(3077844645754772831)
XLA Ops:
  0.6 55.8 %shard_map.119 = (bf16[1,128,1024]{2,1,0:T(8,128)(2,1)}, bf16[1,128,512]{2,1,0:T(8,128)(2,1)}, bf16[1,128,512]{2,1,0:T(8,128)(2,1)}, bf16[1,128,512]{2,1,0:T(8,128)(2,1)}, f32[4,16]{1,0:T(4,128)}) custom-call(bf16[1,128,512]{2,1,0:T(8,128)(2,1)} %q_in.1, bf16[1,128,512]{2,1,0:T(8,128)(2,1)} %k_in.1, bf16[1,128,512]{2,1,0:T(8,128)(2,1)} %v_in.1, ...), custom_call_target="tpu_custom_call" | custom-call | tf_op jit(solution)/shard_map/pallas_call | solution.py:514
  56.4 2.0 %shard_map.120 = (bf16[1,128,1024]{2,1,0:T(8,128)(2,1)}, bf16[1,128,512]{2,1,0:T(8,128)(2,1)}, bf16[1,128,512]{2,1,0:T(8,128)(2,1)}, bf16[1,128,512]{2,1,0:T(8,128)(2,1)}, f32[4,16]{1,0:T(4,128)}) custom-call(bf16[1,128,1024]{2,1,0:T(8,128)(2,1)} %get-tuple-element.10.refs_0_, bf16[1,128,512]{2,1,0:T(8,128)(2,1)} %get-tuple-element.11.refs_1_, ...), custom_call_target="tpu_custom_call" | custom-call | tf_op jit(solution)/shard_map/pallas_call | solution.py:541
